TPU v7x, 256 devices: a whole 4x4x8 slice. The times are simulated.
256 devices in a mesh: chan: 32 (over y_lo, z, core), stn: 8 (over y_hi, x).
Axes of the slice: x: 4, y: 4 (y_hi: 2, y_lo: 2; y = y_hi * 2 + y_lo), z: 8, core: 2. Of those that a mesh axis runs over, the one named last changes fastest.
Arguments:
- volts: bfloat16 [1024, 2, 98304], P('stn', None, 'chan'), may hold values from -6 to 6
- taps: float32 [16, 256], replicated, may hold values from -1.5 to 1.5
Outputs:
- visibilities: float32 [256, 2, 1024, 1024], P(('chan', 'stn'))
All inputs are finite; a program needn't handle non-finite values.
Results may differ from a plain program's by a relative error of at most 0.0035.
Values may be sent and summed in bfloat16 or wider, within the bound.
A program may use at most 128 MiB of HBM per device.

v0:
```python
import math

import jax
import jax.numpy as jnp
from jax import lax
from jax.sharding import PartitionSpec as P


def passed_along(block, axis, distance):
    devices = range(lax.axis_size(axis))
    route = [(i - distance, i) for i in devices if i - distance in devices]
    return lax.ppermute(block, axis, route)


def fourier_table(length):
    positions = jnp.arange(length, dtype=jnp.int32)
    phases = positions[:, None] * positions[None, :] % length
    angles = phases.astype(jnp.float32) * (2.0 * math.pi / length)
    cosine = jnp.cos(angles) / math.sqrt(length)
    sine_part = jnp.sin(angles) / math.sqrt(length)
    upper_rows = jnp.concatenate([cosine, sine_part], axis=1)
    lower_rows = jnp.concatenate([-sine_part, cosine], axis=1)
    return jnp.concatenate([upper_rows, lower_rows], axis=0)


def shards(volts, taps):
    local_inputs = volts.shape[0]
    samples = volts.shape[2]
    tap_count, length = taps.shape
    spec_dev = samples // length
    history_len = (tap_count - 1) * length
    reach_count = (tap_count - 2) // spec_dev + 1
    received = jnp.zeros((local_inputs, 2, history_len), volts.dtype)
    for repeat in range(reach_count):
        buffer = jnp.concatenate([received, volts], axis=2)[:, :, samples:]
        received = passed_along(buffer, "chan", 1)
    joined = jnp.concatenate([received, volts], axis=2)
    shaped = joined.reshape(local_inputs, 2, spec_dev + tap_count - 1, length)
    filtered = jnp.zeros((local_inputs, 2, spec_dev, length), jnp.float32)
    for tap_index in range(tap_count):
        begin = tap_count - 1 - tap_index
        filtered = filtered + taps[tap_index] * shaped[:, :, begin : begin + spec_dev, :].astype(
            jnp.float32
        )
    stacked = filtered.transpose(0, 2, 1, 3).reshape(local_inputs, spec_dev, 2 * length)
    fourier = fourier_table(length)
    spectra = jnp.einsum("kl,isl->kis", fourier, stacked, precision=lax.Precision.HIGHEST).astype(
        jnp.bfloat16
    )
    chan_count = lax.axis_size("chan")
    stn_count = lax.axis_size("stn")
    per_device = length // (chan_count * stn_count)
    arranged = spectra.reshape(2, chan_count, stn_count, per_device, local_inputs * spec_dev)
    turned = lax.all_to_all(
        lax.all_to_all(arranged, "chan", split_axis=1, concat_axis=1, tiled=True),
        "stn",
        split_axis=2,
        concat_axis=2,
        tiled=True,
    )
    inputs = stn_count * local_inputs
    total = chan_count * spec_dev
    fields = turned.reshape(2, chan_count, stn_count, per_device, local_inputs, spec_dev)
    fields = fields.transpose(3, 0, 2, 4, 1, 5).reshape(per_device, 2, inputs, total)
    real_part = fields[:, 0]
    imag_part = fields[:, 1]
    right_rows = jnp.concatenate([real_part, imag_part], axis=2)
    lower_rows = jnp.concatenate([imag_part, -real_part], axis=2)
    left_rows = jnp.concatenate([right_rows, lower_rows], axis=1)
    product = jnp.einsum("fat,fbt->fab", left_rows, right_rows, preferred_element_type=jnp.float32)
    return product.reshape(per_device, 2, inputs, inputs) / total


def solution(mesh):
    placed = (P("stn", None, "chan"), P())
    return jax.shard_map(
        shards,
        mesh=mesh,
        in_specs=placed,
        out_specs=P(("chan", "stn"), None, None, None),
        check_vma=False,
    )
```

profile of v0, /device:TPU:1, one launch (start us, length us, event | category | flops | bytes accessed | tf_op | source)
XLA Modules:
  0.0 229.9 jit_solution(5998033511211334366)
XLA Ops:
  0.0 3.7 %copy.22 = bf16[128,2,3072]{0,2,1:T(8,128)(2,1)S(1)} copy(bf16[128,2,3072]{2,1,0:T(2,128)(2,1)} %param.2) | data formatting | bytes 3145728 | tf_op args[0]
  3.7 0.0 copy-start
  3.7 0.1 pad_slice_fusion
  3.9 0.0 copy-start.1
  3.9 5.1 %collective-permute-start = (bf16[128,2,3840]{0,2,1:T(8,128)(2,1)S(1)}, bf16[128,2,3840]{0,2,1:T(8,128)(2,1)S(1)}, u32[]{:S(2)}, u32[]{:S(2)}) collective-permute-start(bf16[128,2,3840]{0,2,1:T(8,128)(2,1)S(1)} %pad_slice_fusion), channel_id=1, source_target_pairs={{0,8},{8,16},{16,24},{24,32},{32,40},{40,48},{48,56},{56,64},{64,7... | collective-permute-start | bytes 5898248 | tf_op jit(solution)/shard_map/ppermute | solution.py:12
  9.0 21.6 %collective-permute-done = bf16[128,2,3840]{0,2,1:T(8,128)(2,1)S(1)} collective-permute-done((bf16[128,2,3840]{0,2,1:T(8,128)(2,1)S(1)}, bf16[128,2,3840]{0,2,1:T(8,128)(2,1)S(1)}, u32[]{:S(2)}, u32[]{:S(2)}) %collective-permute-start) | collective-permute-done | bytes 1966112 | tf_op jit(solution)/shard_map/ppermute | solution.py:12
  30.5 0.1 pad_maximum_fusion.1
  30.6 0.0 copy-done
  30.7 4.4 %collective-permute-start.1 = (bf16[128,2,3840]{0,2,1:T(8,128)(2,1)S(1)}, bf16[128,2,3840]{0,2,1:T(8,128)(2,1)S(1)}, u32[]{:S(2)}, u32[]{:S(2)}) collective-permute-start(bf16[128,2,3840]{0,2,1:T(8,128)(2,1)S(1)} %pad_maximum_fusion.1), channel_id=1, source_target_pairs={{0,8},{8,16},{16,24},{24,32},{32,40},{40,48},{48,56},{56,64},{64,7... | collective-permute-start | bytes 5898248 | tf_op jit(solution)/shard_map/ppermute | solution.py:12
  35.0 1.0 fusion.14
  36.0 1.1 sine_multiply_fusion
  37.1 0.0 copy-done.1
  37.1 19.5 %collective-permute-done.1 = bf16[128,2,3840]{0,2,1:T(8,128)(2,1)S(1)} collective-permute-done((bf16[128,2,3840]{0,2,1:T(8,128)(2,1)S(1)}, bf16[128,2,3840]{0,2,1:T(8,128)(2,1)S(1)}, u32[]{:S(2)}, u32[]{:S(2)}) %collective-permute-start.1) | collective-permute-done | bytes 1966112 | tf_op jit(solution)/shard_map/ppermute | solution.py:12
  56.6 1.6 pad_maximum_fusion
  58.2 6.6 %add_bitcast_fusion = f32[128,12,2,256]{0,3,1,2:T(8,128)S(1)} fusion(bf16[128,2,27,256]{0,3,2,1:T(8,128)(2,1)S(1)} %bitcast.42, f32[256]{0:T(256)S(1)} %bitcast.64, f32[256]{0:T(256)S(1)} %bitcast.65, f32[256]{0:T(256)S(1)} %bitcast.51, f32[256]{0:T(256)S(1)} %bitcast.52, f32[256]{0:T(256)S(1)} %bitcast.53, f32[256]{0:T(256)S(1)} %bitcast.54, ...), kind=kLoop, calls=%fused_computation.4 | loop fusion | flops 36962304 | bytes 28327936 | tf_op jit(solution)/shard_map/transpose | solution.py:45
  64.9 0.2 copy.25
  65.1 6.3 %convolution_convert_fusion = bf16[512,128,12]{1,0,2:T(8,128)(2,1)} fusion(f32[128,12,512]{0,2,1:T(8,128)S(1)} %bitcast.44, f32[256,256]{1,0:T(8,128)S(1)} %get-tuple-element.24, f32[256,256]{1,0:T(8,128)S(1)} %fusion.14, f32[256,256]{1,0:T(8,128)S(1)} %get-tuple-element.23), kind=kOutput, calls=%fused_computation.6 | convolution fusion | flops 4833411072 | bytes 5505024 | tf_op jit(solution)/shard_map/kl,isl->kis/dot_general | solution.py:47
  71.5 12.6 %copy.27 = bf16[512,128,12]{2,1,0:T(8,128)(2,1)} copy(bf16[512,128,12]{1,0,2:T(8,128)(2,1)} %convolution_convert_fusion) | data formatting | bytes 3145728 | tf_op jit(solution)/shard_map/convert_element_type | solution.py:47
  84.0 31.2 %reshape.56 = bf16[2,32,8,1,1536]{4,2,1,0,3:T(8,128)(2,1)S(1)} reshape(bf16[512,128,12]{2,1,0:T(8,128)(2,1)} %copy.27) | data formatting | bytes 3145728 | tf_op jit(solution)/shard_map/reshape | solution.py:53
  115.3 0.2 copy.28
  115.5 51.7 %all_to_all.10 = bf16[2,32,8,1,1536]{4,2,0,3,1:T(8,128)(2,1)S(1)} all-to-all(bf16[2,32,8,1,1536]{4,2,0,3,1:T(8,128)(2,1)S(1)} %copy.28), channel_id=1, replica_groups=mesh['chan'=32,'stn'=8] {'chan'}, dimensions={1} | all-to-all | bytes 3145728 | tf_op jit(solution)/shard_map/all_to_all | solution.py:55
  167.2 0.9 copy.29
  168.1 26.4 %all_to_all.11 = bf16[2,32,8,1,1536]{4,1,0,3,2:T(8,128)(2,1)S(1)} all-to-all(bf16[2,32,8,1,1536]{4,1,0,3,2:T(8,128)(2,1)S(1)} %copy.29), channel_id=1, replica_groups=mesh['chan'=32,'stn'=8] {'stn'}, dimensions={2} | all-to-all | bytes 3145728 | tf_op jit(solution)/shard_map/all_to_all | solution.py:54
  194.5 5.8 %copy.30 = bf16[2,32,8,1,1536]{1,2,4,0,3:T(8,128)(2,1)} copy(bf16[2,32,8,1,1536]{4,1,0,3,2:T(8,128)(2,1)S(1)} %all_to_all.11) | data formatting | bytes 3145728 | tf_op jit(solution)/shard_map/all_to_all | solution.py:54
  200.3 9.8 %copy.31 = bf16[1,2,8,128,32,12]{3,2,5,4,1,0:T(8,128)(2,1)S(1)} copy(bf16[1,2,8,128,32,12]{4,2,5,3,1,0:T(8,128)(2,1)} %bitcast.43) | data formatting | bytes 3145728 | tf_op jit(solution)/shard_map/transpose | solution.py:64
  210.1 0.7 reshape.58
  210.9 0.1 fusion.17
  211.0 0.4 copy.36
  211.4 0.4 copy.35
  211.7 0.1 bitcast_negate_fusion
  211.8 12.3 %maximum_maximum_fusion = bf16[1,2048,768]{2,1,0:T(8,128)(2,1)S(1)} fusion(bf16[1,1024,384]{2,1,0:T(8,128)(2,1)S(1)} %bitcast_negate_fusion, bf16[1,1024,384]{2,1,0:T(8,128)(2,1)S(1)} %bitcast.48, bf16[1,1024,384]{2,1,0:T(8,128)(2,1)S(1)} %bitcast.45), kind=kLoop, calls=%fused_computation.3 | loop fusion | flops 12582912 | bytes 5505024 | tf_op jit(solution)/shard_map/concatenate | solution.py:69
  224.1 5.8 %multiply_bitcast_fusion = f32[1,2,1024,1024]{3,2,1,0:T(8,128)} fusion(bf16[2,1024,768]{2,1,0:T(8,128)(2,1)S(1)} %bitcast.47, bf16[1,1024,384]{2,1,0:T(8,128)(2,1)S(1)} %bitcast.49, bf16[1,1024,384]{2,1,0:T(8,128)(2,1)S(1)} %bitcast.46), kind=kOutput, calls=%fused_computation | convolution fusion | flops 3226468352 | bytes 13107200 | tf_op jit(solution)/shard_map/fat,fbt->fab/dot_general | solution.py:70
  (1 shorter events, 0.0 us)
Async XLA Ops:
  3.7 26.9 %copy-start = (bf16[128,2,3072]{0,2,1:T(8,128)(2,1)}, bf16[128,2,3072]{0,2,1:T(8,128)(2,1)S(1)}, u32[]{:S(2)}) copy-start(bf16[128,2,3072]{0,2,1:T(8,128)(2,1)S(1)} %copy.22) | copy-start | bytes 4718596
  3.9 33.2 %copy-start.1 = (f32[16,256]{1,0:T(8,128)S(1)}, f32[16,256]{1,0:T(8,128)}, u32[]{:S(2)}) copy-start(f32[16,256]{1,0:T(8,128)} %param.3) | copy-start | bytes 49156
  3.9 26.6 %collective-permute-start = (bf16[128,2,3840]{0,2,1:T(8,128)(2,1)S(1)}, bf16[128,2,3840]{0,2,1:T(8,128)(2,1)S(1)}, u32[]{:S(2)}, u32[]{:S(2)}) collective-permute-start(bf16[128,2,3840]{0,2,1:T(8,128)(2,1)S(1)} %pad_slice_fusion), channel_id=1, source_target_pairs={{0,8},{8,16},{16,24},{24,32},{32,40},{40,48},{48,56},{56,64},{64,7... | collective-permute-start | bytes 5898248 | tf_op jit(solution)/shard_map/ppermute | solution.py:12
  30.7 25.9 %collective-permute-start.1 = (bf16[128,2,3840]{0,2,1:T(8,128)(2,1)S(1)}, bf16[128,2,3840]{0,2,1:T(8,128)(2,1)S(1)}, u32[]{:S(2)}, u32[]{:S(2)}) collective-permute-start(bf16[128,2,3840]{0,2,1:T(8,128)(2,1)S(1)} %pad_maximum_fusion.1), channel_id=1, source_target_pairs={{0,8},{8,16},{16,24},{24,32},{32,40},{40,48},{48,56},{56,64},{64,7... | collective-permute-start | bytes 5898248 | tf_op jit(solution)/shard_map/ppermute | solution.py:12
where the time goes:
time: 232 us; the launch traced here: 230 us
  blocking collectives  78.2 us (34%)
  local copies, waits for them, and re-layouts  66.1 us (28%)
  waiting for transfers between devices  41 us (18%)
  other arithmetic  22.8 us (10%)
  matrix products  12.2 us (5%)
  starting transfers between devices  9.46 us (4%)
    all_to_all x1, blocking collectives, shards(): lax.all_to_all(arranged, 'chan', split_axis=1, concat_axis=1, tiled=True)  51.7 us
    ppermute x2, waiting for transfers between devices, passed_along(): return lax.ppermute(block, axis, route)  41 us
    reshape x2, local copies, waits for them, and re-layouts, shards(): spectra.reshape(2, chan_count, stn_count, per_device, local_inputs * spec...  31.4 us
    all_to_all x1, blocking collectives, shards(): lax.all_to_all(lax.all_to_all(arranged, 'chan', split_axis=1, concat_axis...  26.4 us
    convert_element_type x1, local copies, waits for them, and re-layouts, shards(): jnp.einsum('kl,isl->kis', fourier, stacked, precision=lax.Precision.HIGHEST)  12.6 us
    concatenate x1, other arithmetic, shards(): left_rows = jnp.concatenate([right_rows, lower_rows], axis=1)  12.3 us
    transpose x1, local copies, waits for them, and re-layouts, shards(): fields.transpose(3, 0, 2, 4, 1, 5).reshape(per_device, 2, inputs, total)  9.78 us
    ppermute x2, starting transfers between devices, passed_along(): return lax.ppermute(block, axis, route)  9.46 us
  transfers between devices with their start and end apart: 2, of which 2 were waited for; matrix products, arithmetic and copies ran while one was open for 1% of the time, Pallas kernels for 0%

commit v1 on v0

v1 whole, which is shorter than its diff:
```python
import functools
import math

import jax
import jax.numpy as jnp
import numpy as np
from jax import lax
from jax.experimental import pallas as pl
from jax.experimental.pallas import tpu as pltpu
from jax.sharding import PartitionSpec as P

MESH = pl.DeviceIdType.MESH
F32 = jnp.float32
BF16 = jnp.bfloat16

FINE = 256
TAPS = 16
OWN = 12
PRE = 7
POST = 8
LANES = 128
ROWS = 256
GROUP = 8


def fourier_tables():
    index = np.arange(FINE)
    angle = (index[:, None] * index[None, :] % FINE) * (2.0 * math.pi / FINE)
    c, s = np.cos(angle) / math.sqrt(FINE), np.sin(angle) / math.sqrt(FINE)
    whole = np.block([[c, s], [-s, c]]).astype(np.float32)
    high = whole.astype(BF16)
    return high, (whole - high.astype(np.float32)).astype(BF16)


def channelize_kernel(*refs):
    own, fast, slow = refs[:24], refs[24:48], refs[48:64]
    taps, whigh, wlow, stage, window, filtered, xhigh, xlow, turned = refs[64:]
    chan = lax.axis_index("chan")
    core = chan % 2

    def put(at, ref):
        window[at] = ref.reshape(ROWS, LANES)[...]

    def clear(begin, end):
        def step(i, carry):
            window[i] = jnp.zeros((ROWS, LANES), BF16)
            return carry

        lax.fori_loop(begin, end, step, 0)

    @pl.when(core == 0)
    def _():
        for i in range(2 * PRE):
            put(i, slow[2 + i])
        for i in range(24):
            put(2 * PRE + i, own[i])
            put(2 * PRE + 24 + i, fast[i])

    @pl.when(core == 1)
    def _():
        for i in range(6):
            put(i, fast[18 + i])
        for i in range(24):
            put(6 + i, own[i])
        for i in range(2 * POST):
            put(30 + i, slow[i])

    @pl.when(chan == 0)
    def _():
        clear(0, 2 * PRE)

    @pl.when(chan == 31)
    def _():
        clear(0, 30)

    def group(first):
        def filter_rows(i, carry):
            half = i % 2
            rows = pl.ds(pl.multiple_of((i // 2) * 16, 16), 16)
            inputs = [
                window[2 * (first + n) + half, rows, :].astype(F32)
                for n in range(GROUP + TAPS - 1)
            ]
            for j in range(GROUP):
                total = None
                for k in range(TAPS):
                    term = taps[half, pl.ds(k, 1), :] * inputs[j + TAPS - 1 - k]
                    total = term if total is None else total + term
                filtered[half * GROUP + j, rows, :] = total
            return carry

        lax.fori_loop(0, 2 * (ROWS // 16), filter_rows, 0)

        def split(j, carry):
            rows = pl.ds(pl.multiple_of(j * LANES, LANES), LANES)
            for half in range(2):
                for part in range(2):
                    value = filtered[half * GROUP + j, pl.ds(part, LANES, stride=2), :]
                    high = value.astype(BF16)
                    columns = pl.ds((part * 2 + half) * LANES, LANES)
                    xhigh[rows, columns] = high
                    xlow[rows, columns] = (value - high.astype(F32)).astype(BF16)
            return carry

        lax.fori_loop(0, GROUP, split, 0)

        high, low = whigh[...], wlow[...]
        dims = (((1,), (1,)), ((), ()))

        def transform(j, carry):
            inputs = pl.ds(pl.multiple_of(j * 256, 256), 256)
            value = xhigh[inputs, :]
            total = lax.dot_general(high, value, dims, preferred_element_type=F32)
            total += lax.dot_general(low, value, dims, preferred_element_type=F32)
            total += lax.dot_general(high, xlow[inputs, :], dims, preferred_element_type=F32)
            turned[2 * j] = total[:, :LANES]
            turned[2 * j + 1] = total[:, LANES:]
            return carry

        lax.fori_loop(0, GROUP // 2, transform, 0)
        flat = turned.reshape(GROUP * 2 * FINE, LANES)

        def turn(i, carry):
            for n in range(8):
                f = i * 8 + n
                real = flat[pl.ds(f, GROUP, stride=2 * FINE), :]
                imag = flat[pl.ds(FINE + f, GROUP, stride=2 * FINE), :]
                stage[f, 2 * first : 2 * first + 16] = jnp.concatenate([real, imag], axis=0).astype(
                    BF16
                )
            return carry

        lax.fori_loop(0, FINE // 8, turn, 0)

    group(0)

    @pl.when(core == 0)
    def _():
        group(GROUP)

    @pl.when(core == 1)
    def _():
        stage[:, 16:] = jnp.zeros((FINE, 16, LANES), BF16)


def channelize(volts, fast, slow, taps):
    high, low = fourier_tables()
    taps = taps.reshape(TAPS, 2, LANES).transpose(1, 0, 2)
    column = lambda i: pl.BlockSpec((128, 2, LANES), lambda s: (0, 0, i))
    whole = lambda shape: pl.BlockSpec(shape, lambda s: (0,) * len(shape))
    return pl.pallas_call(
        channelize_kernel,
        grid=(1,),
        out_shape=jax.ShapeDtypeStruct((FINE, 32, LANES), BF16),
        in_specs=[column(i) for i in range(24)]
        + [column(i) for i in range(24)]
        + [column(i) for i in range(16)]
        + [whole((2, TAPS, LANES)), whole((512, 512)), whole((512, 512))],
        out_specs=whole((FINE, 32, LANES)),
        scratch_shapes=[
            pltpu.VMEM((62, ROWS, LANES), BF16),
            pltpu.VMEM((2 * GROUP, ROWS, LANES), F32),
            pltpu.VMEM((GROUP * LANES, 2 * FINE), BF16),
            pltpu.VMEM((GROUP * LANES, 2 * FINE), BF16),
            pltpu.VMEM((GROUP, 2 * FINE, LANES), F32),
        ],
        compiler_params=pltpu.CompilerParams(vmem_limit_bytes=48 << 20),
    )(*[volts] * 24, *[fast] * 24, *[slow] * 16, taps, jnp.asarray(high), jnp.asarray(low))


def correlate_kernel(*refs):
    parts, (out, held, turned, crossed) = refs[:8], refs[8:]
    step = pl.program_id(0)
    depth = held.shape[0]

    @pl.when(step == 0)
    def _():
        for g in range(8):
            held[:, g * LANES : (g + 1) * LANES] = parts[g][...].reshape(depth, LANES)
        turned[...] = held[...].T

        def cross(i, carry):
            rows = pl.ds(pl.multiple_of(i * 16, 16), 16)
            block = held[rows, :].astype(F32)
            crossed[rows, :] = jnp.concatenate([-block[8:], block[:8]], axis=0).astype(BF16)
            return carry

        lax.fori_loop(0, depth // 16, cross, 0)

    rows = turned[pl.ds(pl.multiple_of(step * 256, 256), 256), :]
    scale = 1.0 / 384
    out[0, 0] = jnp.dot(rows, held[...], preferred_element_type=F32) * scale
    out[0, 1] = jnp.dot(rows, crossed[...], preferred_element_type=F32) * scale


def correlate(got, shape, part):
    depth = math.prod(shape) // LANES
    return pl.pallas_call(
        correlate_kernel,
        grid=(4,),
        out_shape=jax.ShapeDtypeStruct((1, 2, 1024, 1024), F32),
        in_specs=[pl.BlockSpec(shape, functools.partial(part, g)) for g in range(8)],
        out_specs=pl.BlockSpec((1, 2, 256, 1024), lambda i: (0, 0, i, 0)),
        scratch_shapes=[
            pltpu.VMEM((depth, 1024), BF16),
            pltpu.VMEM((1024, depth), BF16),
            pltpu.VMEM((depth, 1024), BF16),
        ],
        compiler_params=pltpu.CompilerParams(vmem_limit_bytes=48 << 20),
    )(*[got] * 8)


def shards(volts, taps):
    core = lax.axis_index("chan") % 2
    fast = lax.ppermute(volts, "chan", [(i, i ^ 1) for i in range(32)])
    reach = POST * FINE
    edge = jnp.where(core == 0, volts[:, :, :reach], volts[:, :, -reach:])
    slow = lax.ppermute(edge, "chan", [(i, (i + (1 if i % 2 else -1)) % 32) for i in range(32)])
    stage = channelize(volts, fast, slow, taps)
    got = lax.all_to_all(stage, ("chan", "stn"), 0, 0, tiled=True)
    return correlate(
        got.reshape(32, 8, 32, LANES), (32, 1, 32, LANES), lambda g, i: (0, g, 0, 0)
    )


def solution(mesh):
    return jax.shard_map(
        shards,
        mesh=mesh,
        in_specs=(P("stn", None, "chan"), P()),
        out_specs=P(("chan", "stn"), None, None, None),
        check_vma=False,
    )
```

time: 232 us -> 116 us (0.50)
  local copies, waits for them, and re-layouts: 66.1 us -> 0.02 us
  waiting for transfers between devices: 41 us -> 14.5 us
  Pallas kernels: 0 us -> 21.1 us
  other arithmetic: 22.8 us -> 2.41 us
  matrix products: 12.2 us -> 0 us
  starting transfers between devices: 9.46 us -> 3.33 us
  blocking collectives: 78.2 us -> 74.4 us
    reshape x3 -> x0, local copies, waits for them, and re-layouts: 32.1 us -> none  [the longest x2 31.4 us: shards(): spectra.reshape(2, chan_count, stn_count, per_device, local_inputs * spec...]
    ppermute x2, waiting for transfers between devices: 41 us -> 14.5 us  [the longest x1 14.5 us: shards(): lax.ppermute(edge, 'chan', [(i, (i + (1 if i % 2 else -1)) % 32) for i in...]
    pallas_call x0 -> x2, Pallas kernels: none -> 21.1 us  [the longest x1 13.3 us: channelize(): pl.pallas_call(channelize_kernel, grid=(1,), out_shape=jax.ShapeDtypeStru...]
    concatenate x3 -> x0, other arithmetic: 14 us -> none  [the longest x1 12.3 us: shards(): left_rows = jnp.concatenate([right_rows, lower_rows], axis=1)]
    convert_element_type x1 -> x0, local copies, waits for them, and re-layouts: 12.6 us -> none  [shards(): jnp.einsum('kl,isl->kis', fourier, stacked, precision=lax.Precision.HIGHEST)]
    dot_general x2 -> x0, matrix products: 12.2 us -> none  [the longest x1 6.35 us: shards(): jnp.einsum('kl,isl->kis', fourier, stacked, precision=lax.Precision.HIGHEST)]
    transpose x2 -> x1, local copies, waits for them, and re-layouts: 9.99 us -> 0.01 us  [channelize(): taps = taps.reshape(TAPS, 2, LANES).transpose(1, 0, 2)]
    all_to_all x2 -> x0, local copies, waits for them, and re-layouts: 6.71 us -> none  [the longest x1 5.84 us: shards(): lax.all_to_all(lax.all_to_all(arranged, 'chan', split_axis=1, concat_axis...]
  transfers between devices with their start and end apart: 2 -> 2, of which waited for: 2 -> 1; matrix products, arithmetic and copies ran while one was open for 1% -> 2% of each run, Pallas kernels for 0% -> 0%
where the time goes in v1:
time: 116 us
  blocking collectives  74.4 us (64%)
  Pallas kernels  21.1 us (18%)
  waiting for transfers between devices  14.5 us (12%)
  starting transfers between devices  3.33 us (3%)
  other arithmetic  2.41 us (2%)
    all_to_all x1, blocking collectives, shards(): got = lax.all_to_all(stage, ('chan', 'stn'), 0, 0, tiled=True)  74.4 us
    ppermute x1, waiting for transfers between devices, shards(): lax.ppermute(edge, 'chan', [(i, (i + (1 if i % 2 else -1)) % 32) for i in...  14.5 us
    pallas_call x1, Pallas kernels, channelize(): pl.pallas_call(channelize_kernel, grid=(1,), out_shape=jax.ShapeDtypeStru...  13.3 us
    pallas_call x1, Pallas kernels, correlate(): pl.pallas_call(correlate_kernel, grid=(4,), out_shape=jax.ShapeDtypeStruc...  7.78 us
    ppermute x1, starting transfers between devices, shards(): fast = lax.ppermute(volts, 'chan', [(i, i ^ 1) for i in range(32)])  3.24 us
    select_n x1, other arithmetic, shards(): edge = jnp.where(core == 0, volts[:, :, :reach], volts[:, :, -reach:])  2.41 us
  transfers between devices with their start and end apart: 2, of which 1 were waited for; matrix products, arithmetic and copies ran while one was open for 2% of the time, Pallas kernels for 0%

profile of v1, /device:TPU:1, one launch (start us, length us, event | category | flops | bytes accessed | tf_op | source)
XLA Modules:
  0.0 115.7 jit_solution(10112574579628758954)
XLA Ops:
  0.0 0.0 copy-start
  0.0 0.0 copy-start.1
  0.0 3.2 %collective-permute-start = (bf16[128,2,3072]{2,1,0:T(2,128)(2,1)}, bf16[128,2,3072]{2,1,0:T(2,128)(2,1)S(1)}, u32[]{:S(2)}, u32[]{:S(2)}) collective-permute-start(bf16[128,2,3072]{2,1,0:T(2,128)(2,1)} %refs_23_.1), channel_id=1, source_target_pairs={{0,8},{8,0},{16,24},{24,16},{32,40},{40,32},{48,56},{56,48},{64,72... | collective-permute-start | bytes 4718600 | tf_op jit(solution)/shard_map/ppermute | solution.py:215
  3.2 0.0 copy-start.2
  3.2 0.0 copy-start.3
  3.3 2.4 %broadcast_select_fusion = bf16[128,2,2048]{2,1,0:T(2,128)(2,1)S(1)} fusion(pred[]{:T(512)S(6)} %eq.5, bf16[128,2,3072]{2,1,0:T(2,128)(2,1)} %refs_23_.1), kind=kLoop, calls=%fused_computation | loop fusion | flops 524288 | bytes 3145729 | tf_op jit(solution)/shard_map/jit(_where)/select_n | solution.py:217
  5.7 0.1 collective-permute-start.1
  5.8 0.0 copy-done
  5.8 14.5 %collective-permute-done.1.refs_48_.refs_49_.refs_50_.refs_51_.refs_52_.refs_53_.refs_54_.refs_55_.refs_56_.refs_57_.refs_58_.refs_59_.refs_60_.refs_61_.refs_62_.refs_63_ = bf16[128,2,2048]{2,1,0:T(2,128)(2,1)S(1)} collective-permute-done((bf16[128,2,2048]{2,1,0:T(2,128)(2,1)S(1)}, bf16[128,2,2048]{2,1,0:T(2,128)(2,1)S(1)}, u32[]{:S(2)}, u32[]{:S(2)}) %collective-permute-start.1) | collective-permute-done | bytes 1048608 | tf_op jit(solution)/shard_map/ppermute | solution.py:218
  20.3 0.0 collective-permute-done.refs_24_.refs_25_.refs_26_.refs_27_.refs_28_.refs_29_.refs_30_.refs_31_.refs_32_.refs_33_.refs_34_.refs_35_.refs_36_.refs_37_.refs_38_.refs_39_.refs_40_.refs_41_.refs_42_.refs_43_.refs_44_.refs_45_.refs_46_.refs_47_
  20.3 0.0 copy-done.1
  20.3 0.0 copy-done.2
  20.3 0.0 copy-done.3
  20.3 13.3 %shard_map.46 = bf16[256,32,128]{2,1,0:T(8,128)(2,1)} custom-call(bf16[128,2,3072]{2,1,0:T(2,128)(2,1)S(1)} %copy-done.1, bf16[128,2,3072]{2,1,0:T(2,128)(2,1)S(1)} %copy-done.1, bf16[128,2,3072]{2,1,0:T(2,128)(2,1)S(1)} %copy-done.1, bf16[128,2,3072]{2,1,0:T(2,128)(2,1)S(1)} %copy-done.1, bf16[128,2,3072]{2,1,0:T(2,128)(2,1)S(1)} %copy-done.1, ...), custom_call_target="tpu_custom_call" | custom-call | tf_op jit(solution)/shard_map/pallas_call | solution.py:151
  33.6 74.4 %all_to_all.5 = bf16[256,32,128]{2,1,0:T(8,128)(2,1)S(1)} all-to-all(bf16[256,32,128]{2,1,0:T(8,128)(2,1)} %shard_map.46), channel_id=1, replica_groups=mesh['chan'=32,'stn'=8] {'chan','stn'}, dimensions={0} | all-to-all | bytes 4194304 | tf_op jit(solution)/shard_map/all_to_all | solution.py:220
  108.0 7.8 %shard_map.47 = f32[1,2,1024,1024]{3,2,1,0:T(8,128)} custom-call(bf16[32,8,32,128]{3,2,1,0:T(8,128)(2,1)S(1)} %bitcast.8, bf16[32,8,32,128]{3,2,1,0:T(8,128)(2,1)S(1)} %bitcast.9, bf16[32,8,32,128]{3,2,1,0:T(8,128)(2,1)S(1)} %bitcast.10, bf16[32,8,32,128]{3,2,1,0:T(8,128)(2,1)S(1)} %bitcast.11, bf16[32,8,32,128]{3,2,1,0:T(8,128)(2,1)S(1)} %bitcast.12, ...), custom_call_target="tpu_custom_call" | custom-call | tf_op jit(solution)/shard_map/pallas_call | solution.py:198
  (1 shorter events, 0.0 us)
Async XLA Ops:
  0.0 5.8 %copy-start = (f32[16,256]{1,0:T(8,128)S(1)}, f32[16,256]{1,0:T(8,128)}, u32[]{:S(2)}) copy-start(f32[16,256]{1,0:T(8,128)} %param.5) | copy-start | bytes 49156
  0.0 20.3 %copy-start.1 = (bf16[128,2,3072]{2,1,0:T(2,128)(2,1)S(1)}, bf16[128,2,3072]{2,1,0:T(2,128)(2,1)}, u32[]{:S(2)}) copy-start(bf16[128,2,3072]{2,1,0:T(2,128)(2,1)} %refs_23_.1) | copy-start | bytes 4718596
  0.0 20.3 %collective-permute-start = (bf16[128,2,3072]{2,1,0:T(2,128)(2,1)}, bf16[128,2,3072]{2,1,0:T(2,128)(2,1)S(1)}, u32[]{:S(2)}, u32[]{:S(2)}) collective-permute-start(bf16[128,2,3072]{2,1,0:T(2,128)(2,1)} %refs_23_.1), channel_id=1, source_target_pairs={{0,8},{8,0},{16,24},{24,16},{32,40},{40,32},{48,56},{56,48},{64,72... | collective-permute-start | bytes 4718600 | tf_op jit(solution)/shard_map/ppermute | solution.py:215
  3.2 17.0 %copy-start.2 = (bf16[512,512]{1,0:T(8,128)(2,1)S(1)}, bf16[512,512]{1,0:T(8,128)(2,1)}, u32[]{:S(2)}) copy-start(bf16[512,512]{1,0:T(8,128)(2,1)} %constant.25.clone.refs_66_) | copy-start | bytes 1572868
  3.2 17.0 %copy-start.3 = (bf16[512,512]{1,0:T(8,128)(2,1)S(1)}, bf16[512,512]{1,0:T(8,128)(2,1)}, u32[]{:S(2)}) copy-start(bf16[512,512]{1,0:T(8,128)(2,1)} %constant.24.clone.refs_65_) | copy-start | bytes 1572868
  5.7 14.6 %collective-permute-start.1 = (bf16[128,2,2048]{2,1,0:T(2,128)(2,1)S(1)}, bf16[128,2,2048]{2,1,0:T(2,128)(2,1)S(1)}, u32[]{:S(2)}, u32[]{:S(2)}) collective-permute-start(bf16[128,2,2048]{2,1,0:T(2,128)(2,1)S(1)} %broadcast_select_fusion), channel_id=1, source_target_pairs={{0,248},{8,16},{16,8},{24,32},{32,24},{40,48},{48,40},{56,64},{64,... | collective-permute-start | bytes 3145736 | tf_op jit(solution)/shard_map/ppermute | solution.py:218

commit v2 on v1

v2 whole, which is shorter than its diff:
```python
import functools
import math

import jax
import jax.numpy as jnp
import numpy as np
from jax import lax
from jax.experimental import pallas as pl
from jax.experimental.pallas import tpu as pltpu
from jax.sharding import PartitionSpec as P

MESH = pl.DeviceIdType.MESH
F32 = jnp.float32
BF16 = jnp.bfloat16

FINE = 256
TAPS = 16
POST = 8
LANES = 128
ROWS = 256
GROUP = 8
Z_ORDER = (4, 3, 5, 2, 6, 1, 7, 0)


def fourier_tables():
    z, core, y, x = np.unravel_index(np.arange(FINE), (8, 2, 4, 4))
    channel = ((y % 2) * 16 + z * 2 + core) * 8 + (y // 2) * 4 + x
    angle = (channel[:, None] * np.arange(FINE)[None, :] % FINE) * (2.0 * math.pi / FINE)
    c, s = np.cos(angle) / math.sqrt(FINE), np.sin(angle) / math.sqrt(FINE)
    whole = np.block([[c, s], [-s, c]]).astype(np.float32)
    high = whole.astype(BF16)
    return high, (whole - high.astype(np.float32)).astype(BF16)


def filter_group(window, taps, whigh, wlow, stage, filtered, xhigh, xlow, turned):
    def filter_rows(i, carry):
        half = i % 2
        rows = pl.ds(pl.multiple_of((i // 2) * 16, 16), 16)
        inputs = [window[2 * n + half, rows, :].astype(F32) for n in range(GROUP + TAPS - 1)]
        for j in range(GROUP):
            total = None
            for k in range(TAPS):
                term = taps[half, pl.ds(k, 1), :] * inputs[j + TAPS - 1 - k]
                total = term if total is None else total + term
            filtered[half * GROUP + j, rows, :] = total
        return carry

    lax.fori_loop(0, 2 * (ROWS // 16), filter_rows, 0)

    def split(j, carry):
        rows = pl.ds(pl.multiple_of(j * LANES, LANES), LANES)
        for half in range(2):
            for part in range(2):
                value = filtered[half * GROUP + j, pl.ds(part, LANES, stride=2), :]
                high = value.astype(BF16)
                columns = pl.ds((part * 2 + half) * LANES, LANES)
                xhigh[rows, columns] = high
                xlow[rows, columns] = (value - high.astype(F32)).astype(BF16)
        return carry

    lax.fori_loop(0, GROUP, split, 0)

    high, low = whigh[...], wlow[...]
    dims = (((1,), (1,)), ((), ()))

    def transform(j, carry):
        inputs = pl.ds(pl.multiple_of(j * 256, 256), 256)
        value = xhigh[inputs, :]
        total = lax.dot_general(high, value, dims, preferred_element_type=F32)
        total += lax.dot_general(low, value, dims, preferred_element_type=F32)
        total += lax.dot_general(high, xlow[inputs, :], dims, preferred_element_type=F32)
        turned[2 * j] = total[:, :LANES]
        turned[2 * j + 1] = total[:, LANES:]
        return carry

    lax.fori_loop(0, GROUP // 2, transform, 0)
    flat = turned.reshape(GROUP * 2 * FINE, LANES)

    def turn(i, carry):
        for n in range(8):
            f = i * 8 + n
            real = flat[pl.ds(f, GROUP, stride=2 * FINE), :]
            imag = flat[pl.ds(FINE + f, GROUP, stride=2 * FINE), :]
            stage[f] = jnp.concatenate([real, imag], axis=0).astype(BF16)
        return carry

    lax.fori_loop(0, FINE // 8, turn, 0)


def put(window, at, ref):
    window[at] = ref.reshape(ROWS, LANES)[...]


def inner_kernel(*refs):
    own, fast = refs[:22], refs[22:46]
    taps, whigh, wlow, stage, window, *scratch = refs[46:]

    @pl.when(lax.axis_index("chan") % 2 == 0)
    def _():
        for i in range(22):
            put(window, i, own[i])
        for i in range(24):
            put(window, 22 + i, fast[i])
        filter_group(window, taps, whigh, wlow, stage, *scratch)


def edge_kernel(*refs):
    own, fast, slow = refs[:24], refs[24:38], refs[38:54]
    taps, whigh, wlow, stage, window, *scratch = refs[54:]
    chan = lax.axis_index("chan")
    core = chan % 2

    @pl.when(core == 0)
    def _():
        for i in range(14):
            put(window, i, slow[2 + i])
        for i in range(24):
            put(window, 14 + i, own[i])
        for i in range(8):
            put(window, 38 + i, fast[i])

    @pl.when(core == 1)
    def _():
        for i in range(6):
            put(window, i, fast[8 + i])
        for i in range(24):
            put(window, 6 + i, own[i])
        for i in range(16):
            put(window, 30 + i, slow[i])

    def clear(end):
        def step(i, carry):
            window[i] = jnp.zeros((ROWS, LANES), BF16)
            return carry

        lax.fori_loop(0, end, step, 0)

    @pl.when(chan == 0)
    def _():
        clear(14)

    @pl.when(chan == 31)
    def _():
        clear(30)

    filter_group(window, taps, whigh, wlow, stage, *scratch)


def channelize(kernel, columns, tables):
    whole = lambda shape: pl.BlockSpec(shape, lambda s: (0,) * len(shape))
    column = lambda i: pl.BlockSpec((128, 2, LANES), lambda s: (0, 0, i))
    return pl.pallas_call(
        kernel,
        grid=(1,),
        out_shape=jax.ShapeDtypeStruct((FINE, 16, LANES), BF16),
        in_specs=[column(i) for _, i in columns] + [whole(t.shape) for t in tables],
        out_specs=whole((FINE, 16, LANES)),
        scratch_shapes=[
            pltpu.VMEM((46, ROWS, LANES), BF16),
            pltpu.VMEM((2 * GROUP, ROWS, LANES), F32),
            pltpu.VMEM((GROUP * LANES, 2 * FINE), BF16),
            pltpu.VMEM((GROUP * LANES, 2 * FINE), BF16),
            pltpu.VMEM((GROUP, 2 * FINE, LANES), F32),
        ],
        compiler_params=pltpu.CompilerParams(vmem_limit_bytes=40 << 20),
        cost_estimate=pl.CostEstimate(flops=2 << 30, bytes_accessed=16 << 20, transcendentals=0),
    )(*[array for array, _ in columns], *tables)


def spread_kernel(edge, inner, got, middle, send1, recv1, own1, send2, recv2, own2):
    chan, stn = lax.axis_index("chan"), lax.axis_index("stn")
    core, z, ylow = chan % 2, (chan // 2) % 8, chan // 16
    y, x = (stn // 4) * 2 + ylow, stn % 4
    here = y * 4 + x

    def line_device(dz, side):
        return (ylow * 16 + ((z + dz) % 8) * 2 + side, stn)

    def plane_device(i):
        y2, x2 = (y + i // 4) % 4, (x + i) % 4
        return ((y2 % 2) * 16 + z * 2 + core, (y2 // 2) * 4 + x2), y2 * 4 + x2

    barrier = pltpu.get_barrier_semaphore()

    def greet_plane(i, carry):
        pl.semaphore_signal(barrier, inc=1, device_id=plane_device(i)[0], device_id_type=MESH)
        return carry

    for dz in range(8):
        for turn in range(2):
            if dz or turn:
                device = line_device(dz, (core + turn) % 2)
                pl.semaphore_signal(barrier, inc=1, device_id=device, device_id_type=MESH)
    lax.fori_loop(1, 16, greet_plane, 0)
    pl.semaphore_wait(barrier, 30)

    def block(array, dz, side, row, sem):
        start = (((z + dz) % 8) * 2 + side) * 16
        return dict(
            src_ref=array.at[pl.ds(start, 16)],
            dst_ref=middle.at[z, :, pl.ds(row, 16), :],
            send_sem=send1.at[sem],
            recv_sem=recv1.at[sem],
            device_id=line_device(dz, side),
            device_id_type=MESH,
        )

    def blocks(mine, dz):
        out = []
        for side in range(2):
            if dz or side != mine:
                cross = side != mine
                out.append((edge, side, 32 * mine, dz * 6 + mine * 2 + cross))
                if mine == 0:
                    out.append((inner, side, 16, dz * 6 + 4 + cross))
        return out

    def own_blocks(mine):
        pairs = [(edge, 32 * mine)] + ([(inner, 16)] if mine == 0 else [])
        start = (z * 2 + mine) * 16
        return [
            pltpu.make_async_copy(
                array.at[pl.ds(start, 16)], middle.at[z, :, pl.ds(row, 16), :], own1.at[n]
            )
            for n, (array, row) in enumerate(pairs)
        ]

    for mine in range(2):

        @pl.when(core == mine)
        def _(mine=mine):
            for copy in own_blocks(mine):
                copy.start()
            for dz in Z_ORDER:
                for array, side, row, sem in blocks(mine, dz):
                    pltpu.make_async_remote_copy(**block(array, dz, side, row, sem)).start()

    def arrived(mine, dz):
        for source in range(2):
            for array, side, row, sem in blocks(source, dz):
                if side == mine:
                    pltpu.make_async_remote_copy(**block(array, dz, side, row, sem)).wait_recv()

    for dz in Z_ORDER:
        for mine in range(2):

            @pl.when(core == mine)
            def _(mine=mine, dz=dz):
                arrived(mine, dz)
                if dz == 0:
                    for copy in own_blocks(mine):
                        copy.wait()

        source = (z + 8 - dz) % 8

        def forward(i, carry, source=source):
            device, there = plane_device(i)
            pltpu.make_async_remote_copy(
                src_ref=middle.at[source, there],
                dst_ref=got.at[stn, ylow * 8 + source],
                send_sem=send2,
                recv_sem=recv2,
                device_id=device,
                device_id_type=MESH,
            ).start()
            return carry

        lax.fori_loop(1, 16, forward, 0)

    own = pltpu.make_async_copy(middle.at[:, here], got.at[stn, pl.ds(ylow * 8, 8)], own2)
    own.start()
    for mine in range(2):

        @pl.when(core == mine)
        def _(mine=mine):
            for dz in Z_ORDER:
                for array, side, row, sem in blocks(mine, dz):
                    pltpu.make_async_remote_copy(**block(array, dz, side, row, sem)).wait_send()

    own.wait()
    plane = middle.at[:, pl.ds(0, 15)]
    every = pltpu.make_async_remote_copy(
        src_ref=plane,
        dst_ref=plane,
        send_sem=send2,
        recv_sem=recv2,
        device_id=line_device(1, core),
        device_id_type=MESH,
    )
    every.wait_send()
    every.wait_recv()


def spread(edge, inner):
    any_spec = pl.BlockSpec(memory_space=pl.ANY)
    dma = pltpu.SemaphoreType.DMA
    return pl.pallas_call(
        spread_kernel,
        out_shape=jax.ShapeDtypeStruct((8, 16, 48, LANES), BF16),
        in_specs=[any_spec, any_spec],
        out_specs=any_spec,
        scratch_shapes=[
            pltpu.VMEM((8, 16, 48, LANES), BF16),
            dma((48,)),
            dma((48,)),
            dma((2,)),
            dma,
            dma,
            dma,
        ],
        compiler_params=pltpu.CompilerParams(
            collective_id=0, has_side_effects=True, vmem_limit_bytes=16 << 20
        ),
    )(edge, inner)


def correlate_kernel(*refs):
    parts, (out, held, turned, crossed) = refs[:8], refs[8:]
    step = pl.program_id(0)
    depth = held.shape[0]

    @pl.when(step == 0)
    def _():
        for g in range(8):
            held[:, g * LANES : (g + 1) * LANES] = parts[g][...].reshape(depth, LANES)
        turned[...] = held[...].T

        def cross(i, carry):
            rows = pl.ds(pl.multiple_of(i * 16, 16), 16)
            block = held[rows, :].astype(F32)
            crossed[rows, :] = jnp.concatenate([-block[8:], block[:8]], axis=0).astype(BF16)
            return carry

        lax.fori_loop(0, depth // 16, cross, 0)

    rows = turned[pl.ds(pl.multiple_of(step * 256, 256), 256), :]
    scale = 1.0 / 384
    out[0, 0] = jnp.dot(rows, held[...], preferred_element_type=F32) * scale
    out[0, 1] = jnp.dot(rows, crossed[...], preferred_element_type=F32) * scale


def correlate(got, shape, part):
    depth = math.prod(shape) // LANES
    return pl.pallas_call(
        correlate_kernel,
        grid=(4,),
        out_shape=jax.ShapeDtypeStruct((1, 2, 1024, 1024), F32),
        in_specs=[pl.BlockSpec(shape, functools.partial(part, g)) for g in range(8)],
        out_specs=pl.BlockSpec((1, 2, 256, 1024), lambda i: (0, 0, i, 0)),
        scratch_shapes=[
            pltpu.VMEM((depth, 1024), BF16),
            pltpu.VMEM((1024, depth), BF16),
            pltpu.VMEM((depth, 1024), BF16),
        ],
        compiler_params=pltpu.CompilerParams(vmem_limit_bytes=48 << 20),
    )(*[got] * 8)


def shards(volts, taps):
    core = lax.axis_index("chan") % 2
    reach = POST * FINE
    edge = jnp.where(core == 0, volts[:, :, :reach], volts[:, :, -reach:])
    slow = lax.ppermute(edge, "chan", [(i, (i + (1 if i % 2 else -1)) % 32) for i in range(32)])
    fast = lax.ppermute(volts, "chan", [(i, i ^ 1) for i in range(32)])
    high, low = fourier_tables()
    taps = taps.reshape(TAPS, 2, LANES).transpose(1, 0, 2)
    tables = (taps, jnp.asarray(high), jnp.asarray(low))
    inner = channelize(
        inner_kernel,
        [(volts, i) for i in range(2, 24)] + [(fast, i) for i in range(24)],
        tables,
    )
    near = list(range(8)) + list(range(18, 24))
    outer = channelize(
        edge_kernel,
        [(volts, i) for i in range(24)]
        + [(fast, i) for i in near]
        + [(slow, i) for i in range(16)],
        tables,
    )
    got = spread(outer, inner)
    return correlate(got, (1, 16, 48, LANES), lambda g, i: (g, 0, 0, 0))


def solution(mesh):
    return jax.shard_map(
        shards,
        mesh=mesh,
        in_specs=(P("stn", None, "chan"), P()),
        out_specs=P(("chan", "stn"), None, None, None),
        check_vma=False,
    )
```

time: 116 us -> 93.1 us (0.80)
  blocking collectives: 74.4 us -> 0 us
  Pallas kernels: 21.1 us -> 74.8 us
  waiting for transfers between devices: 14.5 us -> 12.3 us
    all_to_all x1 -> x0, blocking collectives: 74.4 us -> none  [shards(): got = lax.all_to_all(stage, ('chan', 'stn'), 0, 0, tiled=True)]
    pallas_call x1 -> x3, Pallas kernels: 13.3 us -> 68.3 us  [the longest x1 54.7 us: spread(): pl.pallas_call(spread_kernel, out_shape=jax.ShapeDtypeStruct((8, 16, 48,...]
    ppermute x1, waiting for transfers between devices: 14.5 us -> 11.7 us  [shards(): lax.ppermute(edge, 'chan', [(i, (i + (1 if i % 2 else -1)) % 32) for i in...]
    pallas_call x1, Pallas kernels: 7.78 us -> 6.46 us  [correlate(): pl.pallas_call(correlate_kernel, grid=(4,), out_shape=jax.ShapeDtypeStruc...]
  transfers between devices with their start and end apart: 2 -> 2, of which waited for: 1 -> 2; matrix products, arithmetic and copies ran while one was open for 2% -> 3% of each run, Pallas kernels for 0% -> 2%
where the time goes in v2:
time: 93.1 us; the launch traced here: 93 us
  Pallas kernels  74.8 us (80%)
  waiting for transfers between devices  12.3 us (13%)
  starting transfers between devices  3.33 us (4%)
  other arithmetic  2.47 us (3%)
    pallas_call x1, Pallas kernels, spread(): pl.pallas_call(spread_kernel, out_shape=jax.ShapeDtypeStruct((8, 16, 48,...  54.7 us
    pallas_call x2, Pallas kernels, channelize(): pl.pallas_call(kernel, grid=(1,), out_shape=jax.ShapeDtypeStruct((FINE, 1...  13.6 us
    ppermute x1, waiting for transfers between devices, shards(): lax.ppermute(edge, 'chan', [(i, (i + (1 if i % 2 else -1)) % 32) for i in...  11.7 us
    pallas_call x1, Pallas kernels, correlate(): pl.pallas_call(correlate_kernel, grid=(4,), out_shape=jax.ShapeDtypeStruc...  6.46 us
    ppermute x1, starting transfers between devices, shards(): fast = lax.ppermute(volts, 'chan', [(i, i ^ 1) for i in range(32)])  3.24 us
    select_n x1, other arithmetic, shards(): edge = jnp.where(core == 0, volts[:, :, :reach], volts[:, :, -reach:])  2.47 us
  transfers between devices with their start and end apart: 2, of which 2 were waited for; matrix products, arithmetic and copies ran while one was open for 3% of the time, Pallas kernels for 2%

profile of v2, /device:TPU:1, one launch (start us, length us, event | category | flops | bytes accessed | tf_op | source)
XLA Modules:
  0.0 93.0 jit_solution(14228019379036936825)
XLA Ops:
  0.0 0.0 copy-start
  0.0 3.2 %collective-permute-start = (bf16[128,2,3072]{2,1,0:T(2,128)(2,1)}, bf16[128,2,3072]{2,1,0:T(2,128)(2,1)S(1)}, u32[]{:S(2)}, u32[]{:S(2)}) collective-permute-start(bf16[128,2,3072]{2,1,0:T(2,128)(2,1)} %refs_21_.3), channel_id=1, source_target_pairs={{0,8},{8,0},{16,24},{24,16},{32,40},{40,32},{48,56},{56,48},{64,72... | collective-permute-start | bytes 4718600 | tf_op jit(solution)/shard_map/ppermute | solution.py:364
  3.2 0.0 copy-start.1
  3.2 0.0 copy-start.2
  3.2 0.0 copy-start.3
  3.3 2.5 %broadcast_select_fusion = bf16[128,2,2048]{2,1,0:T(2,128)(2,1)S(1)} fusion(pred[]{:T(512)S(6)} %eq.5, bf16[128,2,3072]{2,1,0:T(2,128)(2,1)} %refs_21_.3), kind=kLoop, calls=%fused_computation | loop fusion | flops 524288 | bytes 3145729 | tf_op jit(solution)/shard_map/jit(_where)/select_n | solution.py:362
  5.7 0.1 collective-permute-start.1
  5.8 0.0 copy-done
  5.9 0.6 collective-permute-done.refs_24_.refs_25_.refs_26_.refs_27_.refs_28_.refs_29_.refs_30_.refs_31_.refs_32_.refs_33_.refs_34_.refs_35_.refs_36_.refs_37_.refs_22_.refs_23_.refs_38_.refs_39_.refs_40_.refs_41_.refs_42_.refs_43_.refs_44_.refs_45_
  6.5 0.0 copy-done.1
  6.5 0.0 copy-done.2
  6.5 0.0 copy-done.3
  6.5 2.1 %shard_map.47.inner = bf16[256,16,128]{2,1,0:T(8,128)(2,1)S(1)} custom-call(bf16[128,2,3072]{2,1,0:T(2,128)(2,1)S(1)} %copy-done.1, bf16[128,2,3072]{2,1,0:T(2,128)(2,1)S(1)} %copy-done.1, bf16[128,2,3072]{2,1,0:T(2,128)(2,1)S(1)} %copy-done.1, bf16[128,2,3072]{2,1,0:T(2,128)(2,1)S(1)} %copy-done.1, bf16[128,2,3072]{2,1,0:T(2,128)(2,1)S(1)} %copy-done.1, ...), custom_call_target="tpu_custom_call" | custom-call | flops 2147483648 | bytes 16777216 | tf_op jit(solution)/shard_map/pallas_call | solution.py:152
  8.6 11.7 %collective-permute-done.1.refs_38_.refs_39_.refs_40_.refs_41_.refs_42_.refs_43_.refs_44_.refs_45_.refs_46_.refs_47_.refs_48_.refs_49_.refs_50_.refs_51_.refs_52_.refs_53_ = bf16[128,2,2048]{2,1,0:T(2,128)(2,1)S(1)} collective-permute-done((bf16[128,2,2048]{2,1,0:T(2,128)(2,1)S(1)}, bf16[128,2,2048]{2,1,0:T(2,128)(2,1)S(1)}, u32[]{:S(2)}, u32[]{:S(2)}) %collective-permute-start.1) | collective-permute-done | bytes 1048608 | tf_op jit(solution)/shard_map/ppermute | solution.py:363
  20.3 11.4 %shard_map.46.edge = bf16[256,16,128]{2,1,0:T(8,128)(2,1)S(1)} custom-call(bf16[128,2,3072]{2,1,0:T(2,128)(2,1)S(1)} %copy-done.1, bf16[128,2,3072]{2,1,0:T(2,128)(2,1)S(1)} %copy-done.1, bf16[128,2,3072]{2,1,0:T(2,128)(2,1)S(1)} %copy-done.1, bf16[128,2,3072]{2,1,0:T(2,128)(2,1)S(1)} %copy-done.1, bf16[128,2,3072]{2,1,0:T(2,128)(2,1)S(1)} %copy-done.1, ...), custom_call_target="tpu_custom_call" | custom-call | flops 2147483648 | bytes 16777216 | tf_op jit(solution)/shard_map/pallas_call | solution.py:152
  31.8 54.7 %shard_map.48.refs_0_.refs_1_.refs_2_.refs_3_.refs_4_.refs_5_.refs_6_.refs_7_ = bf16[8,16,48,128]{3,2,1,0:T(8,128)(2,1)S(1)} custom-call(bf16[256,16,128]{2,1,0:T(8,128)(2,1)S(1)} %shard_map.46.edge, bf16[256,16,128]{2,1,0:T(8,128)(2,1)S(1)} %shard_map.47.inner), custom_call_target="tpu_custom_call" | custom-call | tf_op jit(solution)/shard_map/pallas_call | solution.py:297
  86.5 6.5 %shard_map.49 = f32[1,2,1024,1024]{3,2,1,0:T(8,128)} custom-call(bf16[8,16,48,128]{3,2,1,0:T(8,128)(2,1)S(1)} %shard_map.48.refs_0_.refs_1_.refs_2_.refs_3_.refs_4_.refs_5_.refs_6_.refs_7_, bf16[8,16,48,128]{3,2,1,0:T(8,128)(2,1)S(1)} %shard_map.48.refs_0_.refs_1_.refs_2_.refs_3_.refs_4_.refs_5_.refs_6_.refs_7_, ...), custom_call_target="tpu_custom_call" | custom-call | tf_op jit(solution)/shard_map/pallas_call | solution.py:344
  (1 shorter events, 0.0 us)
Async XLA Ops:
  0.0 5.8 %copy-start = (f32[16,256]{1,0:T(8,128)S(1)}, f32[16,256]{1,0:T(8,128)}, u32[]{:S(2)}) copy-start(f32[16,256]{1,0:T(8,128)} %param.5) | copy-start | bytes 49156
  0.0 6.5 %collective-permute-start = (bf16[128,2,3072]{2,1,0:T(2,128)(2,1)}, bf16[128,2,3072]{2,1,0:T(2,128)(2,1)S(1)}, u32[]{:S(2)}, u32[]{:S(2)}) collective-permute-start(bf16[128,2,3072]{2,1,0:T(2,128)(2,1)} %refs_21_.3), channel_id=1, source_target_pairs={{0,8},{8,0},{16,24},{24,16},{32,40},{40,32},{48,56},{56,48},{64,72... | collective-permute-start | bytes 4718600 | tf_op jit(solution)/shard_map/ppermute | solution.py:364
  3.2 3.2 %copy-start.1 = (bf16[128,2,3072]{2,1,0:T(2,128)(2,1)S(1)}, bf16[128,2,3072]{2,1,0:T(2,128)(2,1)}, u32[]{:S(2)}) copy-start(bf16[128,2,3072]{2,1,0:T(2,128)(2,1)} %refs_21_.3) | copy-start | bytes 4718596
  3.2 3.3 %copy-start.2 = (bf16[512,512]{1,0:T(8,128)(2,1)S(1)}, bf16[512,512]{1,0:T(8,128)(2,1)}, u32[]{:S(2)}) copy-start(bf16[512,512]{1,0:T(8,128)(2,1)} %constant.25.clone.refs_56_.refs_48_) | copy-start | bytes 1572868
  3.2 3.3 %copy-start.3 = (bf16[512,512]{1,0:T(8,128)(2,1)S(1)}, bf16[512,512]{1,0:T(8,128)(2,1)}, u32[]{:S(2)}) copy-start(bf16[512,512]{1,0:T(8,128)(2,1)} %constant.24.clone.refs_55_.refs_47_) | copy-start | bytes 1572868
  5.7 14.6 %collective-permute-start.1 = (bf16[128,2,2048]{2,1,0:T(2,128)(2,1)S(1)}, bf16[128,2,2048]{2,1,0:T(2,128)(2,1)S(1)}, u32[]{:S(2)}, u32[]{:S(2)}) collective-permute-start(bf16[128,2,2048]{2,1,0:T(2,128)(2,1)S(1)} %broadcast_select_fusion), channel_id=1, source_target_pairs={{0,248},{8,16},{16,8},{24,32},{32,24},{40,48},{48,40},{56,64},{64,... | collective-permute-start | bytes 3145736 | tf_op jit(solution)/shard_map/ppermute | solution.py:363

commit v3 on v2

--- a/solution.py
+++ b/solution.py
@@ -19,7 +19,8 @@
 LANES = 128
 ROWS = 256
 GROUP = 8
-Z_ORDER = (4, 3, 5, 2, 6, 1, 7, 0)
+Z_ORDER = (0, 4, 3, 5, 2, 6, 1, 7)
+AHEAD = 3
 
 
 def fourier_tables():
@@ -32,33 +33,24 @@
     return high, (whole - high.astype(np.float32)).astype(BF16)
 
 
-def filter_group(window, taps, whigh, wlow, stage, filtered, xhigh, xlow, turned):
+def filter_group(window, taps, whigh, wlow, stage, xhigh, xlow, turned):
     def filter_rows(i, carry):
-        half = i % 2
+        half, part = i % 2, i // 16
         rows = pl.ds(pl.multiple_of((i // 2) * 16, 16), 16)
         inputs = [window[2 * n + half, rows, :].astype(F32) for n in range(GROUP + TAPS - 1)]
+        columns = pl.ds(pl.multiple_of((part * 2 + half) * LANES, LANES), LANES)
         for j in range(GROUP):
             total = None
             for k in range(TAPS):
                 term = taps[half, pl.ds(k, 1), :] * inputs[j + TAPS - 1 - k]
                 total = term if total is None else total + term
-            filtered[half * GROUP + j, rows, :] = total
+            place = pl.ds(pl.multiple_of(j * LANES + (i // 2) % 8 * 16, 16), 16)
+            high = total.astype(BF16)
+            xhigh[place, columns] = high
+            xlow[place, columns] = (total - high.astype(F32)).astype(BF16)
         return carry
 
     lax.fori_loop(0, 2 * (ROWS // 16), filter_rows, 0)
-
-    def split(j, carry):
-        rows = pl.ds(pl.multiple_of(j * LANES, LANES), LANES)
-        for half in range(2):
-            for part in range(2):
-                value = filtered[half * GROUP + j, pl.ds(part, LANES, stride=2), :]
-                high = value.astype(BF16)
-                columns = pl.ds((part * 2 + half) * LANES, LANES)
-                xhigh[rows, columns] = high
-                xlow[rows, columns] = (value - high.astype(F32)).astype(BF16)
-        return carry
-
-    lax.fori_loop(0, GROUP, split, 0)
 
     high, low = whigh[...], wlow[...]
     dims = (((1,), (1,)), ((), ()))
@@ -87,46 +79,34 @@
     lax.fori_loop(0, FINE // 8, turn, 0)
 
 
-def put(window, at, ref):
-    window[at] = ref.reshape(ROWS, LANES)[...]
-
-
-def inner_kernel(*refs):
-    own, fast = refs[:22], refs[22:46]
-    taps, whigh, wlow, stage, window, *scratch = refs[46:]
-
+def put(window, at, ref, begin, count):
+    for i in range(count):
+        window[at + i] = ref[:, (begin + i) * LANES : (begin + i + 1) * LANES]
+
+
+def inner_kernel(own, fast, taps, whigh, wlow, stage, window, *scratch):
     @pl.when(lax.axis_index("chan") % 2 == 0)
     def _():
-        for i in range(22):
-            put(window, i, own[i])
-        for i in range(24):
-            put(window, 22 + i, fast[i])
+        put(window, 0, own, 2, 22)
+        put(window, 22, fast, 0, 24)
         filter_group(window, taps, whigh, wlow, stage, *scratch)
 
 
-def edge_kernel(*refs):
-    own, fast, slow = refs[:24], refs[24:38], refs[38:54]
-    taps, whigh, wlow, stage, window, *scratch = refs[54:]
+def edge_kernel(own, fast, slow, taps, whigh, wlow, stage, window, *scratch):
     chan = lax.axis_index("chan")
     core = chan % 2
 
     @pl.when(core == 0)
     def _():
-        for i in range(14):
-            put(window, i, slow[2 + i])
-        for i in range(24):
-            put(window, 14 + i, own[i])
-        for i in range(8):
-            put(window, 38 + i, fast[i])
+        put(window, 0, slow, 2, 14)
+        put(window, 14, own, 0, 24)
+        put(window, 38, fast, 0, 8)
 
     @pl.when(core == 1)
     def _():
-        for i in range(6):
-            put(window, i, fast[8 + i])
-        for i in range(24):
-            put(window, 6 + i, own[i])
-        for i in range(16):
-            put(window, 30 + i, slow[i])
+        put(window, 0, fast, 18, 6)
+        put(window, 6, own, 0, 24)
+        put(window, 30, slow, 0, 16)
 
     def clear(end):
         def step(i, carry):
@@ -146,25 +126,23 @@
     filter_group(window, taps, whigh, wlow, stage, *scratch)
 
 
-def channelize(kernel, columns, tables):
+def channelize(kernel, *arrays):
     whole = lambda shape: pl.BlockSpec(shape, lambda s: (0,) * len(shape))
-    column = lambda i: pl.BlockSpec((128, 2, LANES), lambda s: (0, 0, i))
     return pl.pallas_call(
         kernel,
         grid=(1,),
         out_shape=jax.ShapeDtypeStruct((FINE, 16, LANES), BF16),
-        in_specs=[column(i) for _, i in columns] + [whole(t.shape) for t in tables],
+        in_specs=[whole(array.shape) for array in arrays],
         out_specs=whole((FINE, 16, LANES)),
         scratch_shapes=[
             pltpu.VMEM((46, ROWS, LANES), BF16),
-            pltpu.VMEM((2 * GROUP, ROWS, LANES), F32),
             pltpu.VMEM((GROUP * LANES, 2 * FINE), BF16),
             pltpu.VMEM((GROUP * LANES, 2 * FINE), BF16),
             pltpu.VMEM((GROUP, 2 * FINE, LANES), F32),
         ],
         compiler_params=pltpu.CompilerParams(vmem_limit_bytes=40 << 20),
         cost_estimate=pl.CostEstimate(flops=2 << 30, bytes_accessed=16 << 20, transcendentals=0),
-    )(*[array for array, _ in columns], *tables)
+    )(*arrays)
 
 
 def spread_kernel(edge, inner, got, middle, send1, recv1, own1, send2, recv2, own2):
@@ -225,15 +203,19 @@
             for n, (array, row) in enumerate(pairs)
         ]
 
-    for mine in range(2):
-
-        @pl.when(core == mine)
-        def _(mine=mine):
-            for copy in own_blocks(mine):
-                copy.start()
-            for dz in Z_ORDER:
-                for array, side, row, sem in blocks(mine, dz):
-                    pltpu.make_async_remote_copy(**block(array, dz, side, row, sem)).start()
+    def start(n):
+        for mine in range(2):
+
+            @pl.when(core == mine)
+            def _(mine=mine):
+                if n == 0:
+                    for copy in own_blocks(mine):
+                        copy.start()
+                for array, side, row, sem in blocks(mine, Z_ORDER[n]):
+                    pltpu.make_async_remote_copy(**block(array, Z_ORDER[n], side, row, sem)).start()
+
+    for n in range(AHEAD):
+        start(n)
 
     def arrived(mine, dz):
         for source in range(2):
@@ -241,7 +223,7 @@
                 if side == mine:
                     pltpu.make_async_remote_copy(**block(array, dz, side, row, sem)).wait_recv()
 
-    for dz in Z_ORDER:
+    for n, dz in enumerate(Z_ORDER):
         for mine in range(2):
 
             @pl.when(core == mine)
@@ -266,6 +248,8 @@
             return carry
 
         lax.fori_loop(1, 16, forward, 0)
+        if n + AHEAD < 8:
+            start(n + AHEAD)
 
     own = pltpu.make_async_copy(middle.at[:, here], got.at[stn, pl.ds(ylow * 8, 8)], own2)
     own.start()
@@ -359,25 +343,16 @@
 def shards(volts, taps):
     core = lax.axis_index("chan") % 2
     reach = POST * FINE
-    edge = jnp.where(core == 0, volts[:, :, :reach], volts[:, :, -reach:])
+    by_part = lambda array: array.transpose(1, 0, 2).reshape(ROWS, -1)
+    own = by_part(volts)
+    edge = jnp.where(core == 0, own[:, :reach], own[:, -reach:])
     slow = lax.ppermute(edge, "chan", [(i, (i + (1 if i % 2 else -1)) % 32) for i in range(32)])
-    fast = lax.ppermute(volts, "chan", [(i, i ^ 1) for i in range(32)])
+    fast = lax.ppermute(own, "chan", [(i, i ^ 1) for i in range(32)])
     high, low = fourier_tables()
     taps = taps.reshape(TAPS, 2, LANES).transpose(1, 0, 2)
     tables = (taps, jnp.asarray(high), jnp.asarray(low))
-    inner = channelize(
-        inner_kernel,
-        [(volts, i) for i in range(2, 24)] + [(fast, i) for i in range(24)],
-        tables,
-    )
-    near = list(range(8)) + list(range(18, 24))
-    outer = channelize(
-        edge_kernel,
-        [(volts, i) for i in range(24)]
-        + [(fast, i) for i in near]
-        + [(slow, i) for i in range(16)],
-        tables,
-    )
+    inner = channelize(inner_kernel, own, fast, *tables)
+    outer = channelize(edge_kernel, own, fast, slow, *tables)
     got = spread(outer, inner)
     return correlate(got, (1, 16, 48, LANES), lambda g, i: (g, 0, 0, 0))
 

time: 93.1 us -> 87 us (0.934)
  Pallas kernels: 74.8 us -> 66.8 us
  other arithmetic: 2.47 us -> 0.09 us
  waiting for transfers between devices: 12.3 us -> 14.5 us
  local copies, waits for them, and re-layouts: 0.02 us -> 1.77 us
    pallas_call x2, Pallas kernels: 13.6 us -> 7.76 us  [channelize(): pl.pallas_call(kernel, grid=(1,), out_shape=jax.ShapeDtypeStruct((FINE, 1...]
    select_n x1, other arithmetic: 2.47 us -> 0.09 us  [shards(): edge = jnp.where(core == 0, own[:, :reach], own[:, -reach:])]
    pallas_call x1, Pallas kernels: 54.7 us -> 52.6 us  [spread(): pl.pallas_call(spread_kernel, out_shape=jax.ShapeDtypeStruct((8, 16, 48,...]
    ppermute x1, waiting for transfers between devices: 0.64 us -> 2.82 us  [shards(): fast = lax.ppermute(own, 'chan', [(i, i ^ 1) for i in range(32)])]
    transpose x0 -> x1, local copies, waits for them, and re-layouts: none -> 1.75 us  [shards(): by_part = lambda array: array.transpose(1, 0, 2).reshape(ROWS, -1)]
  transfers between devices with their start and end apart: 2 -> 2, of which waited for: 2 -> 2; matrix products, arithmetic and copies ran while one was open for 3% -> 0% of each run, Pallas kernels for 2% -> 0%
where the time goes in v3:
time: 87 us; the launch traced here: 86.6 us
  Pallas kernels  66.8 us (77%)
  waiting for transfers between devices  14.5 us (17%)
  starting transfers between devices  3.42 us (4%)
  local copies, waits for them, and re-layouts  1.77 us (2%)
    pallas_call x1, Pallas kernels, spread(): pl.pallas_call(spread_kernel, out_shape=jax.ShapeDtypeStruct((8, 16, 48,...  52.6 us
    ppermute x1, waiting for transfers between devices, shards(): lax.ppermute(edge, 'chan', [(i, (i + (1 if i % 2 else -1)) % 32) for i in...  11.7 us
    pallas_call x2, Pallas kernels, channelize(): pl.pallas_call(kernel, grid=(1,), out_shape=jax.ShapeDtypeStruct((FINE, 1...  7.76 us
    pallas_call x1, Pallas kernels, correlate(): pl.pallas_call(correlate_kernel, grid=(4,), out_shape=jax.ShapeDtypeStruc...  6.46 us
    ppermute x1, starting transfers between devices, shards(): fast = lax.ppermute(own, 'chan', [(i, i ^ 1) for i in range(32)])  3.33 us
    ppermute x1, waiting for transfers between devices, shards(): fast = lax.ppermute(own, 'chan', [(i, i ^ 1) for i in range(32)])  2.82 us
    transpose x1, local copies, waits for them, and re-layouts, shards(): by_part = lambda array: array.transpose(1, 0, 2).reshape(ROWS, -1)  1.75 us
  transfers between devices with their start and end apart: 2, of which 2 were waited for; matrix products, arithmetic and copies ran while one was open for 0% of the time, Pallas kernels for 0%

profile of v3, /device:TPU:1, one launch (start us, length us, event | category | flops | bytes accessed | tf_op | source)
XLA Modules:
  0.0 86.6 jit_solution(15366970471846093433)
XLA Ops:
  0.0 0.0 copy-start
  0.0 1.8 %copy.6 = bf16[2,128,3072]{2,1,0:T(8,128)(2,1)S(1)} copy(bf16[2,128,3072]{2,0,1:T(2,128)(2,1)} %bitcast.13) | data formatting | bytes 3145728 | tf_op jit(solution)/shard_map/transpose | solution.py:346
  1.8 3.3 %collective-permute-start = (bf16[256,3072]{1,0:T(8,128)(2,1)S(1)}, bf16[256,3072]{1,0:T(8,128)(2,1)S(1)}, u32[]{:S(2)}, u32[]{:S(2)}) collective-permute-start(bf16[256,3072]{1,0:T(8,128)(2,1)S(1)} %bitcast.9), channel_id=1, source_target_pairs={{0,8},{8,0},{16,24},{24,16},{32,40},{40,32},{48,56},{56,48},{64,72... | collective-permute-start | bytes 4718600 | tf_op jit(solution)/shard_map/ppermute | solution.py:350
  5.1 0.0 copy-start.1
  5.1 0.0 copy-start.2
  5.1 0.1 slice_select_fusion
  5.2 0.1 collective-permute-start.1
  5.3 0.0 copy-done
  5.3 2.8 %collective-permute-done.fast = bf16[256,3072]{1,0:T(8,128)(2,1)S(1)} collective-permute-done((bf16[256,3072]{1,0:T(8,128)(2,1)S(1)}, bf16[256,3072]{1,0:T(8,128)(2,1)S(1)}, u32[]{:S(2)}, u32[]{:S(2)}) %collective-permute-start) | collective-permute-done | bytes 1572896 | tf_op jit(solution)/shard_map/ppermute | solution.py:350
  8.1 0.0 copy-done.1
  8.1 0.0 copy-done.2
  8.1 11.7 %collective-permute-done.1.slow = bf16[256,2048]{1,0:T(8,128)(2,1)S(1)} collective-permute-done((bf16[256,2048]{1,0:T(8,128)(2,1)S(1)}, bf16[256,2048]{1,0:T(8,128)(2,1)S(1)}, u32[]{:S(2)}, u32[]{:S(2)}) %collective-permute-start.1) | collective-permute-done | bytes 1048608 | tf_op jit(solution)/shard_map/ppermute | solution.py:349
  19.8 7.8 %shard_map.46.edge = bf16[256,16,128]{2,1,0:T(8,128)(2,1)S(1)} custom-call(bf16[256,3072]{1,0:T(8,128)(2,1)S(1)} %bitcast.12, bf16[256,3072]{1,0:T(8,128)(2,1)S(1)} %collective-permute-done.fast, bf16[256,2048]{1,0:T(8,128)(2,1)S(1)} %collective-permute-done.1.slow, f32[2,16,128]{2,1,0:T(8,128)S(1)} %bitcast_bitcast_fusion.taps, ...), custom_call_target="tpu_custom_call" | custom-call | flops 2147483648 | bytes 16777216 | tf_op jit(solution)/shard_map/pallas_call | solution.py:131
  27.6 52.6 %shard_map.48.refs_0_.refs_1_.refs_2_.refs_3_.refs_4_.refs_5_.refs_6_.refs_7_ = bf16[8,16,48,128]{3,2,1,0:T(8,128)(2,1)S(1)} custom-call(bf16[256,16,128]{2,1,0:T(8,128)(2,1)S(1)} %shard_map.46.edge, bf16[256,16,128]{2,1,0:T(8,128)(2,1)S(1)} %shard_map.47.inner), custom_call_target="tpu_custom_call" | custom-call | tf_op jit(solution)/shard_map/pallas_call | solution.py:281
  80.1 6.5 %shard_map.49 = f32[1,2,1024,1024]{3,2,1,0:T(8,128)} custom-call(bf16[8,16,48,128]{3,2,1,0:T(8,128)(2,1)S(1)} %shard_map.48.refs_0_.refs_1_.refs_2_.refs_3_.refs_4_.refs_5_.refs_6_.refs_7_, bf16[8,16,48,128]{3,2,1,0:T(8,128)(2,1)S(1)} %shard_map.48.refs_0_.refs_1_.refs_2_.refs_3_.refs_4_.refs_5_.refs_6_.refs_7_, ...), custom_call_target="tpu_custom_call" | custom-call | tf_op jit(solution)/shard_map/pallas_call | solution.py:328
  (2 shorter events, 0.0 us)
Async XLA Ops:
  0.0 5.3 %copy-start = (f32[16,256]{1,0:T(8,128)S(1)}, f32[16,256]{1,0:T(8,128)}, u32[]{:S(2)}) copy-start(f32[16,256]{1,0:T(8,128)} %param.5) | copy-start | bytes 49156
  1.8 6.4 %collective-permute-start = (bf16[256,3072]{1,0:T(8,128)(2,1)S(1)}, bf16[256,3072]{1,0:T(8,128)(2,1)S(1)}, u32[]{:S(2)}, u32[]{:S(2)}) collective-permute-start(bf16[256,3072]{1,0:T(8,128)(2,1)S(1)} %bitcast.9), channel_id=1, source_target_pairs={{0,8},{8,0},{16,24},{24,16},{32,40},{40,32},{48,56},{56,48},{64,72... | collective-permute-start | bytes 4718600 | tf_op jit(solution)/shard_map/ppermute | solution.py:350
  5.1 3.0 %copy-start.1 = (bf16[512,512]{1,0:T(8,128)(2,1)S(1)}, bf16[512,512]{1,0:T(8,128)(2,1)}, u32[]{:S(2)}) copy-start(bf16[512,512]{1,0:T(8,128)(2,1)} %constant.25.clone.wlow) | copy-start | bytes 1572868
  5.1 3.0 %copy-start.2 = (bf16[512,512]{1,0:T(8,128)(2,1)S(1)}, bf16[512,512]{1,0:T(8,128)(2,1)}, u32[]{:S(2)}) copy-start(bf16[512,512]{1,0:T(8,128)(2,1)} %constant.24.clone.whigh) | copy-start | bytes 1572868
  5.2 14.6 %collective-permute-start.1 = (bf16[256,2048]{1,0:T(8,128)(2,1)S(1)}, bf16[256,2048]{1,0:T(8,128)(2,1)S(1)}, u32[]{:S(2)}, u32[]{:S(2)}) collective-permute-start(bf16[256,2048]{1,0:T(8,128)(2,1)S(1)} %slice_select_fusion), channel_id=1, source_target_pairs={{0,248},{8,16},{16,8},{24,32},{32,24},{40,48},{48,40},{56,64},{64,... | collective-permute-start | bytes 3145736 | tf_op jit(solution)/shard_map/ppermute | solution.py:349

commit v4 on v3

--- a/solution.py
+++ b/solution.py
@@ -19,12 +19,11 @@
 LANES = 128
 ROWS = 256
 GROUP = 8
-Z_ORDER = (0, 4, 3, 5, 2, 6, 1, 7)
-AHEAD = 3
+AHEAD = 2
 
 
 def fourier_tables():
-    z, core, y, x = np.unravel_index(np.arange(FINE), (8, 2, 4, 4))
+    y, x, z, core = np.unravel_index(np.arange(FINE), (4, 4, 8, 2))
     channel = ((y % 2) * 16 + z * 2 + core) * 8 + (y // 2) * 4 + x
     angle = (channel[:, None] * np.arange(FINE)[None, :] % FINE) * (2.0 * math.pi / FINE)
     c, s = np.cos(angle) / math.sqrt(FINE), np.sin(angle) / math.sqrt(FINE)
@@ -154,125 +153,117 @@
     def line_device(dz, side):
         return (ylow * 16 + ((z + dz) % 8) * 2 + side, stn)
 
-    def plane_device(i):
-        y2, x2 = (y + i // 4) % 4, (x + i) % 4
+    def plane_device(dy, dx):
+        y2, x2 = (y + dy) % 4, (x + dx) % 4
         return ((y2 % 2) * 16 + z * 2 + core, (y2 // 2) * 4 + x2), y2 * 4 + x2
 
     barrier = pltpu.get_barrier_semaphore()
-
-    def greet_plane(i, carry):
-        pl.semaphore_signal(barrier, inc=1, device_id=plane_device(i)[0], device_id_type=MESH)
-        return carry
-
-    for dz in range(8):
-        for turn in range(2):
-            if dz or turn:
-                device = line_device(dz, (core + turn) % 2)
-                pl.semaphore_signal(barrier, inc=1, device_id=device, device_id_type=MESH)
-    lax.fori_loop(1, 16, greet_plane, 0)
+    greet = [line_device(dz, (core + turn) % 2) for dz in range(8) for turn in range(2) if dz or turn]
+    greet += [plane_device(i // 4, i % 4)[0] for i in range(1, 16)]
+    for device in greet:
+        pl.semaphore_signal(barrier, inc=1, device_id=device, device_id_type=MESH)
     pl.semaphore_wait(barrier, 30)
 
-    def block(array, dz, side, row, sem):
-        start = (((z + dz) % 8) * 2 + side) * 16
-        return dict(
-            src_ref=array.at[pl.ds(start, 16)],
-            dst_ref=middle.at[z, :, pl.ds(row, 16), :],
-            send_sem=send1.at[sem],
-            recv_sem=recv1.at[sem],
-            device_id=line_device(dz, side),
-            device_id_type=MESH,
-        )
-
-    def blocks(mine, dz):
+    def plane_copies(mine, dy):
         out = []
-        for side in range(2):
-            if dz or side != mine:
-                cross = side != mine
-                out.append((edge, side, 32 * mine, dz * 6 + mine * 2 + cross))
-                if mine == 0:
-                    out.append((inner, side, 16, dz * 6 + 4 + cross))
+        for dx in range(4):
+            if dy or dx:
+                device, there = plane_device(dy, dx)
+                for n, array in enumerate((edge, inner)[: 2 - mine]):
+                    sem = (dy * 4 + dx) * 2 + n
+                    out.append(
+                        pltpu.make_async_remote_copy(
+                            src_ref=array.at[pl.ds(there * 16, 16)],
+                            dst_ref=middle.at[:, here, pl.ds(16 * n, 16), :],
+                            send_sem=send1.at[sem],
+                            recv_sem=recv1.at[sem],
+                            device_id=device,
+                            device_id_type=MESH,
+                        )
+                    )
         return out
 
     def own_blocks(mine):
-        pairs = [(edge, 32 * mine)] + ([(inner, 16)] if mine == 0 else [])
-        start = (z * 2 + mine) * 16
         return [
             pltpu.make_async_copy(
-                array.at[pl.ds(start, 16)], middle.at[z, :, pl.ds(row, 16), :], own1.at[n]
+                array.at[pl.ds(here * 16, 16)],
+                middle.at[:, here, pl.ds(16 * n, 16), :],
+                own1.at[n],
             )
-            for n, (array, row) in enumerate(pairs)
+            for n, array in enumerate((edge, inner)[: 2 - mine])
         ]
 
-    def start(n):
-        for mine in range(2):
-
-            @pl.when(core == mine)
-            def _(mine=mine):
-                if n == 0:
-                    for copy in own_blocks(mine):
-                        copy.start()
-                for array, side, row, sem in blocks(mine, Z_ORDER[n]):
-                    pltpu.make_async_remote_copy(**block(array, Z_ORDER[n], side, row, sem)).start()
-
-    for n in range(AHEAD):
-        start(n)
-
-    def arrived(mine, dz):
-        for source in range(2):
-            for array, side, row, sem in blocks(source, dz):
-                if side == mine:
-                    pltpu.make_async_remote_copy(**block(array, dz, side, row, sem)).wait_recv()
-
-    for n, dz in enumerate(Z_ORDER):
-        for mine in range(2):
-
-            @pl.when(core == mine)
-            def _(mine=mine, dz=dz):
-                arrived(mine, dz)
-                if dz == 0:
+    def own_group(mine, dy):
+        source = (y + 4 - dy) % 4
+        return pltpu.make_async_copy(
+            middle.at[z * 2 + mine, pl.ds(source * 4, 4), pl.ds(0, 32 - 16 * mine), :],
+            got.at[
+                pl.ds((source // 2) * 4, 4), (source % 2) * 8 + z, pl.ds(32 * mine, 32 - 16 * mine), :
+            ],
+            own2.at[dy],
+        )
+
+    for mine in range(2):
+
+        @pl.when(core == mine)
+        def _(mine=mine):
+            rows = 32 - 16 * mine
+            for copy in own_blocks(mine):
+                copy.start()
+            for dy in range(AHEAD):
+                for copy in plane_copies(mine, dy):
+                    copy.start()
+            for dy in range(4):
+                for copy in plane_copies(mine, dy):
+                    copy.wait_recv()
+                if dy == 0:
                     for copy in own_blocks(mine):
                         copy.wait()
-
-        source = (z + 8 - dz) % 8
-
-        def forward(i, carry, source=source):
-            device, there = plane_device(i)
-            pltpu.make_async_remote_copy(
-                src_ref=middle.at[source, there],
-                dst_ref=got.at[stn, ylow * 8 + source],
-                send_sem=send2,
-                recv_sem=recv2,
-                device_id=device,
-                device_id_type=MESH,
-            ).start()
-            return carry
-
-        lax.fori_loop(1, 16, forward, 0)
-        if n + AHEAD < 8:
-            start(n + AHEAD)
-
-    own = pltpu.make_async_copy(middle.at[:, here], got.at[stn, pl.ds(ylow * 8, 8)], own2)
-    own.start()
-    for mine in range(2):
-
-        @pl.when(core == mine)
-        def _(mine=mine):
-            for dz in Z_ORDER:
-                for array, side, row, sem in blocks(mine, dz):
-                    pltpu.make_async_remote_copy(**block(array, dz, side, row, sem)).wait_send()
-
-    own.wait()
-    plane = middle.at[:, pl.ds(0, 15)]
-    every = pltpu.make_async_remote_copy(
-        src_ref=plane,
-        dst_ref=plane,
-        send_sem=send2,
-        recv_sem=recv2,
-        device_id=line_device(1, core),
-        device_id_type=MESH,
-    )
-    every.wait_send()
-    every.wait_recv()
+                source = (y + 4 - dy) % 4
+
+                def forward(i, carry, source=source):
+                    dz, side = (i // 2) * 3 % 8, (core + i) % 2
+                    z2 = (z + dz) % 8
+                    pltpu.make_async_remote_copy(
+                        src_ref=middle.at[
+                            z2 * 2 + side, pl.ds(source * 4, 4), pl.ds(0, rows), :
+                        ],
+                        dst_ref=got.at[
+                            pl.ds((source // 2) * 4, 4),
+                            (source % 2) * 8 + z,
+                            pl.ds(32 * mine, rows),
+                            :,
+                        ],
+                        send_sem=send2,
+                        recv_sem=recv2.at[mine],
+                        device_id=line_device(dz, side),
+                        device_id_type=MESH,
+                    ).start()
+                    return carry
+
+                lax.fori_loop(1, 16, forward, 0)
+                own_group(mine, dy).start()
+                if dy + AHEAD < 4:
+                    for copy in plane_copies(mine, dy + AHEAD):
+                        copy.start()
+            for dy in range(4):
+                for copy in plane_copies(mine, dy):
+                    copy.wait_send()
+                own_group(mine, dy).wait()
+
+            def all_of(ref, sem):
+                return pltpu.make_async_remote_copy(
+                    src_ref=ref,
+                    dst_ref=ref,
+                    send_sem=send2,
+                    recv_sem=recv2.at[sem],
+                    device_id=line_device(1, core),
+                    device_id_type=MESH,
+                )
+
+            all_of(middle.at[pl.ds(0, 15), :, pl.ds(0, rows), :], 0).wait_send()
+            all_of(middle.at[pl.ds(0, 7 + mine)], 0).wait_recv()
+            all_of(middle.at[pl.ds(0, 8 - mine), :, pl.ds(0, 16), :], 1).wait_recv()
 
 
 def spread(edge, inner):
@@ -284,13 +275,13 @@
         in_specs=[any_spec, any_spec],
         out_specs=any_spec,
         scratch_shapes=[
-            pltpu.VMEM((8, 16, 48, LANES), BF16),
-            dma((48,)),
-            dma((48,)),
+            pltpu.VMEM((16, 16, 32, LANES), BF16),
+            dma((32,)),
+            dma((32,)),
             dma((2,)),
             dma,
-            dma,
-            dma,
+            dma((2,)),
+            dma((4,)),
         ],
         compiler_params=pltpu.CompilerParams(
             collective_id=0, has_side_effects=True, vmem_limit_bytes=16 << 20

time: 87 us -> 85.3 us (0.980)
  Pallas kernels: 66.8 us -> 65.4 us
    pallas_call x1, Pallas kernels: 52.6 us -> 51.2 us  [spread(): pl.pallas_call(spread_kernel, out_shape=jax.ShapeDtypeStruct((8, 16, 48,...]
where the time goes in v4:
time: 85.3 us; the launch traced here: 85.2 us
  Pallas kernels  65.4 us (77%)
  waiting for transfers between devices  14.5 us (17%)
  starting transfers between devices  3.42 us (4%)
  local copies, waits for them, and re-layouts  1.77 us (2%)
    pallas_call x1, Pallas kernels, spread(): pl.pallas_call(spread_kernel, out_shape=jax.ShapeDtypeStruct((8, 16, 48,...  51.2 us
    ppermute x1, waiting for transfers between devices, shards(): lax.ppermute(edge, 'chan', [(i, (i + (1 if i % 2 else -1)) % 32) for i in...  11.7 us
    pallas_call x2, Pallas kernels, channelize(): pl.pallas_call(kernel, grid=(1,), out_shape=jax.ShapeDtypeStruct((FINE, 1...  7.76 us
    pallas_call x1, Pallas kernels, correlate(): pl.pallas_call(correlate_kernel, grid=(4,), out_shape=jax.ShapeDtypeStruc...  6.46 us
    ppermute x1, starting transfers between devices, shards(): fast = lax.ppermute(own, 'chan', [(i, i ^ 1) for i in range(32)])  3.33 us
    ppermute x1, waiting for transfers between devices, shards(): fast = lax.ppermute(own, 'chan', [(i, i ^ 1) for i in range(32)])  2.82 us
    transpose x1, local copies, waits for them, and re-layouts, shards(): by_part = lambda array: array.transpose(1, 0, 2).reshape(ROWS, -1)  1.75 us
  transfers between devices with their start and end apart: 2, of which 2 were waited for; matrix products, arithmetic and copies ran while one was open for 0% of the time, Pallas kernels for 0%

profile of v4, /device:TPU:1, one launch (start us, length us, event | category | flops | bytes accessed | tf_op | source)
XLA Modules:
  0.0 85.2 jit_solution(14185743266801402760)
XLA Ops:
  0.0 0.0 copy-start
  0.0 1.8 %copy.6 = bf16[2,128,3072]{2,1,0:T(8,128)(2,1)S(1)} copy(bf16[2,128,3072]{2,0,1:T(2,128)(2,1)} %bitcast.13) | data formatting | bytes 3145728 | tf_op jit(solution)/shard_map/transpose | solution.py:337
  1.8 3.3 %collective-permute-start = (bf16[256,3072]{1,0:T(8,128)(2,1)S(1)}, bf16[256,3072]{1,0:T(8,128)(2,1)S(1)}, u32[]{:S(2)}, u32[]{:S(2)}) collective-permute-start(bf16[256,3072]{1,0:T(8,128)(2,1)S(1)} %bitcast.9), channel_id=1, source_target_pairs={{0,8},{8,0},{16,24},{24,16},{32,40},{40,32},{48,56},{56,48},{64,72... | collective-permute-start | bytes 4718600 | tf_op jit(solution)/shard_map/ppermute | solution.py:341
  5.1 0.0 copy-start.1
  5.1 0.0 copy-start.2
  5.1 0.1 slice_select_fusion
  5.2 0.1 collective-permute-start.1
  5.3 0.0 copy-done
  5.3 2.8 %collective-permute-done.fast = bf16[256,3072]{1,0:T(8,128)(2,1)S(1)} collective-permute-done((bf16[256,3072]{1,0:T(8,128)(2,1)S(1)}, bf16[256,3072]{1,0:T(8,128)(2,1)S(1)}, u32[]{:S(2)}, u32[]{:S(2)}) %collective-permute-start) | collective-permute-done | bytes 1572896 | tf_op jit(solution)/shard_map/ppermute | solution.py:341
  8.1 0.0 copy-done.1
  8.1 0.0 copy-done.2
  8.1 11.7 %collective-permute-done.1.slow = bf16[256,2048]{1,0:T(8,128)(2,1)S(1)} collective-permute-done((bf16[256,2048]{1,0:T(8,128)(2,1)S(1)}, bf16[256,2048]{1,0:T(8,128)(2,1)S(1)}, u32[]{:S(2)}, u32[]{:S(2)}) %collective-permute-start.1) | collective-permute-done | bytes 1048608 | tf_op jit(solution)/shard_map/ppermute | solution.py:340
  19.8 7.8 %shard_map.46.edge = bf16[256,16,128]{2,1,0:T(8,128)(2,1)S(1)} custom-call(bf16[256,3072]{1,0:T(8,128)(2,1)S(1)} %bitcast.12, bf16[256,3072]{1,0:T(8,128)(2,1)S(1)} %collective-permute-done.fast, bf16[256,2048]{1,0:T(8,128)(2,1)S(1)} %collective-permute-done.1.slow, f32[2,16,128]{2,1,0:T(8,128)S(1)} %bitcast_bitcast_fusion.taps, ...), custom_call_target="tpu_custom_call" | custom-call | flops 2147483648 | bytes 16777216 | tf_op jit(solution)/shard_map/pallas_call | solution.py:130
  27.6 51.2 %shard_map.48.refs_0_.refs_1_.refs_2_.refs_3_.refs_4_.refs_5_.refs_6_.refs_7_ = bf16[8,16,48,128]{3,2,1,0:T(8,128)(2,1)S(1)} custom-call(bf16[256,16,128]{2,1,0:T(8,128)(2,1)S(1)} %shard_map.46.edge, bf16[256,16,128]{2,1,0:T(8,128)(2,1)S(1)} %shard_map.47.inner), custom_call_target="tpu_custom_call" | custom-call | tf_op jit(solution)/shard_map/pallas_call | solution.py:272
  78.8 6.5 %shard_map.49 = f32[1,2,1024,1024]{3,2,1,0:T(8,128)} custom-call(bf16[8,16,48,128]{3,2,1,0:T(8,128)(2,1)S(1)} %shard_map.48.refs_0_.refs_1_.refs_2_.refs_3_.refs_4_.refs_5_.refs_6_.refs_7_, bf16[8,16,48,128]{3,2,1,0:T(8,128)(2,1)S(1)} %shard_map.48.refs_0_.refs_1_.refs_2_.refs_3_.refs_4_.refs_5_.refs_6_.refs_7_, ...), custom_call_target="tpu_custom_call" | custom-call | tf_op jit(solution)/shard_map/pallas_call | solution.py:319
  (2 shorter events, 0.0 us)
Async XLA Ops:
  0.0 5.3 %copy-start = (f32[16,256]{1,0:T(8,128)S(1)}, f32[16,256]{1,0:T(8,128)}, u32[]{:S(2)}) copy-start(f32[16,256]{1,0:T(8,128)} %param.5) | copy-start | bytes 49156
  1.8 6.4 %collective-permute-start = (bf16[256,3072]{1,0:T(8,128)(2,1)S(1)}, bf16[256,3072]{1,0:T(8,128)(2,1)S(1)}, u32[]{:S(2)}, u32[]{:S(2)}) collective-permute-start(bf16[256,3072]{1,0:T(8,128)(2,1)S(1)} %bitcast.9), channel_id=1, source_target_pairs={{0,8},{8,0},{16,24},{24,16},{32,40},{40,32},{48,56},{56,48},{64,72... | collective-permute-start | bytes 4718600 | tf_op jit(solution)/shard_map/ppermute | solution.py:341
  5.1 3.0 %copy-start.1 = (bf16[512,512]{1,0:T(8,128)(2,1)S(1)}, bf16[512,512]{1,0:T(8,128)(2,1)}, u32[]{:S(2)}) copy-start(bf16[512,512]{1,0:T(8,128)(2,1)} %constant.25.clone.wlow) | copy-start | bytes 1572868
  5.1 3.0 %copy-start.2 = (bf16[512,512]{1,0:T(8,128)(2,1)S(1)}, bf16[512,512]{1,0:T(8,128)(2,1)}, u32[]{:S(2)}) copy-start(bf16[512,512]{1,0:T(8,128)(2,1)} %constant.24.clone.whigh) | copy-start | bytes 1572868
  5.2 14.6 %collective-permute-start.1 = (bf16[256,2048]{1,0:T(8,128)(2,1)S(1)}, bf16[256,2048]{1,0:T(8,128)(2,1)S(1)}, u32[]{:S(2)}, u32[]{:S(2)}) collective-permute-start(bf16[256,2048]{1,0:T(8,128)(2,1)S(1)} %slice_select_fusion), channel_id=1, source_target_pairs={{0,248},{8,16},{16,8},{24,32},{32,24},{40,48},{48,40},{56,64},{64,... | collective-permute-start | bytes 3145736 | tf_op jit(solution)/shard_map/ppermute | solution.py:340
